TPU v7x, 32 devices: a whole 2x2x4 slice. The times are simulated.
32 devices in a mesh: parts: 2 (over x), user: 16 (over z, y, core).
Axes of the slice: x: 2, y: 2, z: 4, core: 2. Of those that a mesh axis runs over, the one named last changes fastest.
Arguments:
- user_factors: float32 [32768, 64], P(('parts', 'user')), parts along dimension 0, may hold values from -2 to 2
- item_factors: float32 [16384, 64], P(('parts', 'user')), parts along dimension 0, may hold values from -2 to 2
- ratings: bfloat16 [32, 64, 256, 256], P(('parts', 'user')), parts along dimension 0, may hold values from -6 to 6
- rating_len: int32 [32, 64, 256], P(('parts', 'user')), parts along dimension 0, may hold values from 0 to 256, as said below
- rating_user: int32 [32, 64], P(('parts', 'user')), parts along dimension 0, may hold values from 0 to 3
- rating_item: int32 [32, 64], P(('parts', 'user')), parts along dimension 0, may hold values from 0 to 31
- trust_src: int32 [32, 16, 3], P(('parts', 'user')), parts along dimension 0, may hold values from 0 to 3
- trust_dst: int32 [32, 16, 3], P(('parts', 'user')), parts along dimension 0, may hold values from 0 to 3
- trust_weight: bfloat16 [32, 16, 3, 256, 256], P(('parts', 'user')), parts along dimension 0, may hold values from 0 to 1
Outputs:
- user_grad: float32 [32768, 64], P(('parts', 'user')), parts along dimension 0
- item_grad: float32 [16384, 64], P(('parts', 'user')), parts along dimension 0
There are 2 independent parts, one for each index of `parts`. A program takes and returns all parts, laid end to end along the dimension named above; each array names one. Nothing has to cross between parts.
Inputs may be any that keep to these rules, and one draw needn't show every extreme that they name: rating_len[d, r, a] counts the leading item columns of tile r rated by row a; in every tile some row has all 256 and some has none.
All inputs are finite; a program needn't handle non-finite values.
Results may differ from a plain program's by a relative error of at most 0.0031.
Values may be sent and summed in bfloat16 or wider, within the bound.
A program may use at most 128 MiB of HBM per device.

v0:
```python
import jax
import jax.numpy as jnp
from jax import lax
from jax.sharding import PartitionSpec as P

reg_coef = 0.05
social_coef = 8.0


def body(
    user_factors,
    item_factors,
    ratings,
    rating_len,
    rating_user,
    rating_item,
    trust_src,
    trust_dst,
    trust_weight,
):
    tile_size = ratings.shape[-1]
    width = user_factors.shape[1]
    own_count = user_factors.shape[0] // tile_size
    item_count = item_factors.shape[0] // tile_size
    user_blocks = user_factors.reshape(own_count, tile_size, width)
    user_half = user_blocks.astype(jnp.bfloat16)
    item_half = item_factors.astype(jnp.bfloat16)
    all_items = lax.all_gather(item_half, "user", axis=0, tiled=True).reshape(-1, tile_size, width)
    tile_users = rating_user[0]
    tile_items = rating_item[0]
    tile_lengths = rating_len[0]
    user_rows = user_half[tile_users]
    item_rows = all_items[tile_items]
    predicted = jnp.einsum("rak,rbk->rab", user_rows, item_rows, preferred_element_type=jnp.float32)
    columns = lax.broadcasted_iota(jnp.int32, predicted.shape, 2)
    rated = columns < tile_lengths[:, :, None]
    errors = jnp.where(rated, predicted - ratings[0].astype(jnp.float32), 0.0).astype(jnp.bfloat16)
    user_terms = jnp.einsum("rab,rbk->rak", errors, item_rows, preferred_element_type=jnp.float32)
    local_ids = jnp.arange(own_count, dtype=jnp.int32)
    choose = (tile_users[:, None] == local_ids[None, :]).astype(jnp.float32)
    own_terms = jnp.einsum("rc,rak->cak", choose, user_terms)
    item_terms = jnp.einsum("rab,rak->rbk", errors, user_rows, preferred_element_type=jnp.float32)
    target = jnp.arange(item_count * lax.axis_size("user"), dtype=jnp.int32)
    select = (tile_items[:, None] == target[None, :]).astype(jnp.float32)
    item_sum = lax.psum_scatter(
        jnp.einsum("rc,rbk->cbk", select, item_terms), "user", scatter_dimension=0, tiled=True
    )
    truster_ids = trust_src[0]
    trustee_ids = trust_dst[0]
    weights = trust_weight[0]
    wanted = lax.all_to_all(trustee_ids, "user", split_axis=0, concat_axis=0, tiled=True)
    fetched = lax.all_to_all(user_half[wanted], "user", split_axis=0, concat_axis=0, tiled=True)
    tile_sums = jnp.sum(weights, axis=-1, dtype=jnp.float32)
    pick = (truster_ids[:, :, None] == local_ids[None, None, :]).astype(jnp.float32)
    denominator = 1.0 + jnp.einsum("pcu,pca->ua", pick, tile_sums)
    pulled = jnp.einsum("pcab,pcbk->pcak", weights, fetched, preferred_element_type=jnp.float32)
    collected = jnp.einsum("pcu,pcak->uak", pick, pulled)
    pull_error = user_blocks - collected / denominator[:, :, None]
    scaled = (pull_error / denominator[:, :, None]).astype(jnp.bfloat16)
    per_tile = scaled[truster_ids]
    contrib = jnp.einsum("pcab,pcak->pcbk", weights, per_tile, preferred_element_type=jnp.float32)
    arrived = lax.all_to_all(
        contrib.astype(jnp.bfloat16), "user", split_axis=0, concat_axis=0, tiled=True
    ).astype(contrib.dtype)
    placing = (wanted[:, :, None] == local_ids[None, None, :]).astype(jnp.float32)
    returned = jnp.einsum("pcu,pcbk->ubk", placing, arrived)
    user_grad = (
        own_terms + social_coef * pull_error - social_coef * returned + reg_coef * user_blocks
    )
    item_grad = item_sum.reshape(-1, width) + reg_coef * item_factors
    return (user_grad.reshape(-1, width), item_grad)


def solution(mesh):
    in_specs = (
        P(("parts", "user"), None),
        P(("parts", "user"), None),
        P(("parts", "user"), None, None, None),
        P(("parts", "user"), None, None),
        P(("parts", "user"), None),
        P(("parts", "user"), None),
        P(("parts", "user"), None, None),
        P(("parts", "user"), None, None),
        P(("parts", "user"), None, None, None, None),
    )
    out_specs = (P(("parts", "user"), None), P(("parts", "user"), None))
    return jax.shard_map(body, mesh=mesh, in_specs=in_specs, out_specs=out_specs, check_vma=False)
```

profile of v0, /device:TPU:0, one launch (start us, length us, event | category | flops | bytes accessed | tf_op | source)
XLA Modules:
  0.0 175.6 jit_solution(8535734894145844145)
XLA Ops:
  7.2 1.4 copy.63
  8.5 7.4 %all-to-all-start = ((s32[16,1,3]{2,1,0:T(1,128)}), s32[16,1,3]{2,1,0:T(1,128)S(1)}, u32[]{:S(2)}, u32[]{:S(2)}) async-start(s32[16,1,3]{2,1,0:T(1,128)} %copy.63), calls=%async_computation | async-start | bytes 16384 | tf_op jit(solution)/shard_map/all_to_all | solution.py:51
  15.9 0.0 all-gather.2.cloned.1.call-start
  16.0 1.5 convert_element_type.33
  17.5 0.0 all-gather.2.cloned.1.call-update
  17.5 0.7 fusion.62
  18.2 0.7 compare_select_fusion
  18.9 0.7 fusion.63
  19.5 1.1 reshape.140
  20.7 1.6 all-to-all-done
  22.2 0.1 copy.64
  22.3 0.1 copy.65
  22.4 0.1 reshape.163
  22.5 1.9 %gather_fusion.2 = bf16[48,256,64]{1,2,0:T(8,128)(2,1)} fusion(bf16[4,256,64]{1,2,0:T(8,128)(2,1)S(1)} %copy.60, s32[1024]{0:T(1024)S(1)} %pad_clamp_fusion.1), kind=kCustom, calls=%fused_computation.2 | custom fusion | bytes 3145920 | tf_op jit(solution)/shard_map/gather | solution.py:52
  24.4 0.0 copy-start.4
  24.4 4.6 %all-to-all-start.1 = ((bf16[16,3,256,64]{2,3,1,0:T(8,128)(2,1)}), bf16[16,3,256,64]{2,3,1,0:T(8,128)(2,1)}, u32[]{:S(2)}, u32[]{:S(2)}) async-start(bf16[16,3,256,64]{2,3,1,0:T(8,128)(2,1)} %bitcast.11), calls=%async_computation.1 | async-start | bytes 3145728 | tf_op jit(solution)/shard_map/all_to_all | solution.py:52
  29.0 0.0 reduce-scatter.2.cloned.1.call-start
  29.1 0.0 copy-done.4
  29.1 0.1 copy.70
  29.2 0.1 reshape.171
  29.3 0.7 gather_fusion
  30.0 4.5 %convert_reduce_fusion = bf16[16,3,256]{2,1,0:T(4,128)(2,1)S(1)} fusion(bf16[1,16,3,256,256]{4,3,2,1,0:T(8,128)(2,1)} %param.17), kind=kLoop, calls=%fused_computation.8 | loop fusion | flops 6279168 | bytes 6316032 | tf_op jit(solution)/shard_map/reduce_sum | solution.py:53
  34.5 0.2 fusion.41
  34.7 37.0 %all-gather.2.cloned.1.call-done = bf16[8192,64]{0,1:T(8,128)(2,1)} async-done(((bf16[512,64]{0,1:T(8,128)(2,1)}), bf16[8192,64]{0,1:T(8,128)(2,1)}) %all-gather.2.cloned.1.call-update) | async-done | bytes 1048592 | tf_op jit(solution)/shard_map/all_gather | solution.py:28
  71.7 1.3 copy.112
  73.0 0.0 copy-start.7
  73.0 2.0 %gather_fusion.1 = bf16[64,256,64]{1,2,0:T(8,128)(2,1)} fusion(bf16[32,256,64]{1,2,0:T(8,128)(2,1)S(1)} %bitcast.95, s32[1024]{0:T(1024)S(1)} %pad_clamp_fusion.2), kind=kCustom, calls=%fused_computation.1 | custom fusion | bytes 4194560 | tf_op jit(solution)/shard_map/gather | solution.py:33
  75.1 0.0 copy-done.7
  75.1 7.8 %fusion.1 = bf16[64,256,256]{2,1,0:T(8,128)(2,1)S(1)} fusion(bf16[64,256,64]{1,2,0:T(8,128)(2,1)S(1)} %gather_fusion, bf16[64,256,64]{1,2,0:T(8,128)(2,1)} %gather_fusion.1, bf16[1,64,256,256]{3,2,1,0:T(8,128)(2,1)} %param.11, s32[64,256]{1,0:T(8,128)S(1)} %bitcast.108), kind=kOutput, calls=%fused_computation.6 | convolution fusion | flops 557842432 | bytes 21037056 | tf_op jit(solution)/shard_map/rak,rbk->rab/dot_general | solution.py:34
  82.9 0.0 copy-start
  82.9 0.0 copy-start.5
  82.9 1.6 fusion.65
  84.5 1.6 copy-done
  86.1 0.0 copy-done.5
  86.1 1.5 fusion.6
  87.6 2.6 %copy.74 = f32[32,256,64]{1,2,0:T(8,128)} copy(f32[32,256,64]{1,0,2:T(8,128)S(1)} %fusion.6) | data formatting | bytes 4194304 | tf_op jit(solution)/shard_map/rc,rbk->cbk/dot_general | solution.py:46
  90.2 0.0 reduce-scatter.2.cloned.1.call-update
  90.2 0.0 all-to-all-done.1
  90.3 5.3 %fusion.12 = bf16[16,3,256,64]{2,3,1,0:T(8,128)(2,1)S(1)} fusion(bf16[16,3,256,64]{2,3,1,0:T(8,128)(2,1)} %all-to-all-done.1, bf16[1,16,3,256,256]{4,3,2,1,0:T(8,128)(2,1)} %param.17), kind=kOutput, calls=%fused_computation.19 | convolution fusion | flops 402653184 | bytes 9437184 | tf_op jit(solution)/shard_map/pcab,pcbk->pcak/dot_general | solution.py:56
  95.6 1.0 divide_convert_fusion
  96.6 0.7 gather_fusion.3
  97.3 5.3 %fusion.20 = bf16[16,3,256,64]{2,3,1,0:T(8,128)(2,1)} fusion(bf16[16,3,256,64]{2,3,1,0:T(8,128)(2,1)S(1)} %bitcast.96, bf16[1,16,3,256,256]{4,3,2,1,0:T(8,128)(2,1)} %param.17), kind=kOutput, calls=%fused_computation.23 | convolution fusion | flops 403439616 | bytes 9437184 | tf_op jit(solution)/shard_map/pcab,pcak->pcbk/dot_general | solution.py:61
  102.6 0.0 copy-start.1
  102.6 4.7 %all-to-all-start.2 = ((bf16[16,3,256,64]{2,3,1,0:T(8,128)(2,1)}), bf16[16,3,256,64]{2,3,1,0:T(8,128)(2,1)}, u32[]{:S(2)}, u32[]{:S(2)}) async-start(bf16[16,3,256,64]{2,3,1,0:T(8,128)(2,1)} %fusion.20), calls=%async_computation.2 | async-start | bytes 3145728 | tf_op jit(solution)/shard_map/all_to_all | solution.py:62
  107.4 0.1 copy.69
  107.4 0.0 copy-done.1
  107.4 0.0 copy-start.3
  107.4 7.4 %fusion.64 = bf16[64,256,64]{1,2,0:T(8,128)(2,1)} fusion(bf16[64,256,256]{2,1,0:T(8,128)(2,1)} %copy-done, bf16[64,256,64]{1,2,0:T(8,128)(2,1)S(1)} %copy-done.1), kind=kOutput, calls=%fused_computation.62 | convolution fusion | flops 536870912 | bytes 12582912 | tf_op jit(solution)/shard_map/rab,rbk->rak/dot_general | solution.py:38
  114.8 0.0 copy-start.2
  114.8 0.0 copy-start.6
  114.8 47.8 %reduce-scatter.2.cloned.1.call-done = f32[2,256,64]{1,2,0:T(8,128)} async-done(((f32[32,256,64]{1,2,0:T(8,128)}), f32[2,256,64]{1,2,0:T(8,128)}) %reduce-scatter.2.cloned.1.call-update) | async-done | bytes 131088 | tf_op jit(solution)/shard_map/reduce_scatter | solution.py:45
  162.7 0.9 copy.80
  163.6 0.0 copy-done.3
  163.6 0.7 multiply_add_fusion
  164.3 0.0 all-to-all-done.2
  164.3 2.4 %fusion.38 = f32[4,256,64]{1,0,2:T(4,128)S(1)} fusion(bf16[16,3,256,64]{2,3,1,0:T(8,128)(2,1)} %all-to-all-done.2, s32[16,3]{0,1:T(4,128)S(1)} %bitcast.102), kind=kOutput, calls=%fused_computation.29 | convolution fusion | flops 6357184 | bytes 1835200 | tf_op jit(solution)/shard_map/pcu,pcbk->ubk/dot_general | solution.py:66
  166.7 0.0 copy-done.2
  166.7 0.0 copy-done.6
  166.7 1.3 fusion.29
  168.0 0.8 copy.81
  (9 shorter events, 0.1 us)
Async XLA Ops:
  8.5 13.7 %all-to-all-start = ((s32[16,1,3]{2,1,0:T(1,128)}), s32[16,1,3]{2,1,0:T(1,128)S(1)}, u32[]{:S(2)}, u32[]{:S(2)}) async-start(s32[16,1,3]{2,1,0:T(1,128)} %copy.63), calls=%async_computation | async-start | bytes 16384 | tf_op jit(solution)/shard_map/all_to_all | solution.py:51
  15.9 55.8 %all-gather.2.cloned.1.call-start = ((), (), s32[]{:S(2)}) async-start(), calls=%async_computation.4 | async-start | bytes 1114112 | tf_op jit(solution)/shard_map/all_gather | solution.py:28
  24.4 4.7 %copy-start.4 = (s32[1,16,3]{1,0,2:T(1,128)S(1)}, s32[1,16,3]{1,0,2:T(1,128)}, u32[]{:S(2)}) copy-start(s32[1,16,3]{1,0,2:T(1,128)} %param.15) | copy-start | bytes 580
  24.4 65.9 %all-to-all-start.1 = ((bf16[16,3,256,64]{2,3,1,0:T(8,128)(2,1)}), bf16[16,3,256,64]{2,3,1,0:T(8,128)(2,1)}, u32[]{:S(2)}, u32[]{:S(2)}) async-start(bf16[16,3,256,64]{2,3,1,0:T(8,128)(2,1)} %bitcast.11), calls=%async_computation.1 | async-start | bytes 3145728 | tf_op jit(solution)/shard_map/all_to_all | solution.py:52
  29.0 133.6 %reduce-scatter.2.cloned.1.call-start = ((), (), s32[]{:S(2)}) async-start(), calls=%async_computation.5 | async-start | bytes 2228224 | tf_op jit(solution)/shard_map/reduce_scatter | solution.py:45
  73.0 2.0 %copy-start.7 = (s32[1,64,256]{2,1,0:T(8,128)S(1)}, s32[1,64,256]{2,1,0:T(8,128)}, u32[]{:S(2)}) copy-start(s32[1,64,256]{2,1,0:T(8,128)} %param.12) | copy-start | bytes 196612
  82.9 3.2 %copy-start = (bf16[64,256,256]{2,1,0:T(8,128)(2,1)}, bf16[64,256,256]{2,1,0:T(8,128)(2,1)S(1)}, u32[]{:S(2)}) copy-start(bf16[64,256,256]{2,1,0:T(8,128)(2,1)S(1)} %fusion.1) | copy-start | bytes 25165828
  82.9 3.2 %copy-start.5 = (s32[1,64]{1,0:T(1,128)S(1)}, s32[1,64]{1,0:T(1,128)}, u32[]{:S(2)}) copy-start(s32[1,64]{1,0:T(1,128)} %param.14) | copy-start | bytes 772
  102.6 4.8 %copy-start.1 = (bf16[64,256,64]{1,2,0:T(8,128)(2,1)S(1)}, bf16[64,256,64]{1,2,0:T(8,128)(2,1)}, u32[]{:S(2)}) copy-start(bf16[64,256,64]{1,2,0:T(8,128)(2,1)} %gather_fusion.1) | copy-start | bytes 6291460
  102.6 61.6 %all-to-all-start.2 = ((bf16[16,3,256,64]{2,3,1,0:T(8,128)(2,1)}), bf16[16,3,256,64]{2,3,1,0:T(8,128)(2,1)}, u32[]{:S(2)}, u32[]{:S(2)}) async-start(bf16[16,3,256,64]{2,3,1,0:T(8,128)(2,1)} %fusion.20), calls=%async_computation.2 | async-start | bytes 3145728 | tf_op jit(solution)/shard_map/all_to_all | solution.py:62
  107.4 56.1 %copy-start.3 = (f32[512,64]{0,1:T(8,128)S(1)}, f32[512,64]{0,1:T(8,128)}, u32[]{:S(2)}) copy-start(f32[512,64]{0,1:T(8,128)} %param.10) | copy-start | bytes 393220
  114.8 51.9 %copy-start.2 = (bf16[64,256,64]{1,2,0:T(8,128)(2,1)S(1)}, bf16[64,256,64]{1,2,0:T(8,128)(2,1)}, u32[]{:S(2)}) copy-start(bf16[64,256,64]{1,2,0:T(8,128)(2,1)} %fusion.64) | copy-start | bytes 6291460
  114.8 51.9 %copy-start.6 = (s32[1,64]{1,0:T(1,128)S(1)}, s32[1,64]{1,0:T(1,128)}, u32[]{:S(2)}) copy-start(s32[1,64]{1,0:T(1,128)} %param.13) | copy-start | bytes 772
Sparse Core Ops, SparseCore 0:
  19.5 52.1 all-gather.1
  90.4 72.2 reduce-scatter.1
where the time goes:
time: 176 us
  waiting for transfers between devices  86.4 us (49%)
  matrix products  33.9 us (19%)
  starting transfers between devices  16.8 us (10%)
  local copies, waits for them, and re-layouts  15.4 us (9%)
  between operations  14.2 us (8%)
  other arithmetic  8.8 us (5%)
    reduce_scatter x1, waiting for transfers between devices, body(): lax.psum_scatter(jnp.einsum('rc,rbk->cbk', select, item_terms), 'user', s...  47.8 us
    all_gather x1, waiting for transfers between devices, body(): lax.all_gather(item_half, 'user', axis=0, tiled=True)  37 us
    dot_general x1, matrix products, body(): jnp.einsum('rak,rbk->rab', user_rows, item_rows, preferred_element_type=j...  7.81 us
    all_to_all x1, starting transfers between devices, body(): lax.all_to_all(trustee_ids, 'user', split_axis=0, concat_axis=0, tiled=True)  7.39 us
    dot_general x1, matrix products, body(): jnp.einsum('rab,rbk->rak', errors, item_rows, preferred_element_type=jnp....  7.37 us
    dot_general x1, matrix products, body(): jnp.einsum('pcab,pcbk->pcak', weights, fetched, preferred_element_type=jn...  5.33 us
    dot_general x1, matrix products, body(): jnp.einsum('pcab,pcak->pcbk', weights, per_tile, preferred_element_type=j...  5.32 us
    all_to_all x1, starting transfers between devices, body(): lax.all_to_all(contrib.astype(jnp.bfloat16), 'user', split_axis=0, concat...  4.72 us
  transfers between devices with their start and end apart: 5, of which 3 were waited for; matrix products, arithmetic and copies ran while one was open for 29% of the time, Pallas kernels for 0%

commit v1 on v0

v1 whole, which is shorter than its diff:
```python
import functools

import jax
import jax.numpy as jnp
from jax import lax
from jax.experimental import pallas as pl
from jax.experimental.pallas import tpu as pltpu
from jax.sharding import PartitionSpec as P

reg_coef = 0.05
social_coef = 8.0
GROUP = 4
NT = (((1,), (1,)), ((), ()))
F32 = jnp.float32
BF16 = jnp.bfloat16


def kernel(
    n, uf_ref, if_ref, rat_hbm, len_ref, ruser, ritem, tsrc, tdst, w_hbm, links,
    ug_ref, ig_ref,
    rat, w, gi, gu, unat, utf, itf, uto, lens, run, uacc, pacc, pe, scaled,
    ci, ric, riy, riu, rid, cu, ruc, ruy, ruu, rud, own_i, own_u,
    load_sem, agi_s, agi_r, agu_s, agu_r,
    ici_s, ici_r, iy_s, iy_r, iz_s, iz_r,
    uci_s, uci_r, uy_s, uy_r, uz_s, uz_r,
):
    me = lax.axis_index("user")
    H = n // 4
    z = me // 4
    y = (me // 2) % 2
    c = me % 2
    oc = 1 - c
    oy = 1 - y
    T = uf_ref.shape[0] // unat.shape[0]
    K = uf_ref.shape[1]
    ub = unat.shape[0]
    ib = if_ref.shape[0] // T
    R = rat.shape[0]
    cap = w.shape[0] // n

    def at(zz, yy, cc):
        return zz * 4 + yy * 2 + cc

    core = at(z, y, oc)
    side = at(z, oy, c)
    up = at(z + 1, y, c)
    down = at(z - 1, y, c)
    has_up = z < H - 1
    has_down = z > 0

    def remote(src, dst, s, r, dev):
        return pltpu.make_async_remote_copy(
            src_ref=src, dst_ref=dst, send_sem=s, recv_sem=r,
            device_id={"user": dev}, device_id_type=pl.DeviceIdType.MESH,
        )

    loads = []
    parts = 4
    for q in range(parts):
        rows = pl.ds(q * (R // parts), R // parts)
        loads.append(pltpu.make_async_copy(rat_hbm.at[0, rows], rat.at[rows], load_sem.at[q]))
    for q in range(parts):
        rows = pl.ds(q * (n // parts), n // parts)
        wide = pl.ds(q * (n * cap // parts), n * cap // parts)
        loads.append(pltpu.make_async_copy(w_hbm.at[wide], w.at[wide], load_sem.at[parts + q]))

    for b in range(ib):
        t = jnp.transpose(if_ref[pl.ds(b * T, T), :])
        itf[pl.ds(b * K, K), :] = t
        gi[me * ib + b] = t.astype(BF16)

    barrier = pltpu.get_barrier_semaphore()

    def greet(dev):
        pl.semaphore_signal(barrier, inc=1, device_id={"user": dev}, device_id_type=pl.DeviceIdType.MESH)

    greet(core)
    greet(side)

    @pl.when(has_up)
    def _():
        greet(up)

    @pl.when(has_down)
    def _():
        greet(down)

    pl.semaphore_wait(barrier, 2 + has_up.astype(jnp.int32) + has_down.astype(jnp.int32))

    class Gather:
        def __init__(self, buf, width, s, r):
            self.buf, self.width, self.s, self.r = buf, width, s, r

        def copy(self, o, way, dev):
            part = self.buf.at[pl.ds(o * self.width, self.width)]
            return remote(part, part, self.s.at[way, o], self.r.at[o], dev)

        def first(self):
            @pl.when(has_up)
            def _():
                self.copy(me, 0, up).start()

            @pl.when(has_down)
            def _():
                self.copy(me, 1, down).start()

            self.copy(me, 2, side).start()
            self.copy(me, 3, core).start()

        def from_side(self, zz):
            o = at(zz, oy, c)
            self.copy(o, 3, side).wait_recv()
            self.copy(o, 3, core).start()

        def step(self, t):
            @pl.when(z - t >= 0)
            def _():
                o = at(z - t, y, c)
                self.copy(o, 0, core).wait_recv()

                @pl.when(has_up)
                def _():
                    self.copy(o, 0, up).start()

                self.copy(o, 2, side).start()
                self.copy(o, 3, core).start()

            @pl.when(z + t < H)
            def _():
                o = at(z + t, y, c)
                self.copy(o, 1, core).wait_recv()

                @pl.when(has_down)
                def _():
                    self.copy(o, 1, down).start()

                self.copy(o, 2, side).start()
                self.copy(o, 3, core).start()

            self.late(t - 1)

        def late(self, t):
            @pl.when(z - t >= 0)
            def _():
                self.from_side(z - t)

            @pl.when(jnp.logical_and(z + t < H, t > 0))
            def _():
                self.from_side(z + t)

        def finish(self):
            self.late(H - 1)

            def arrive(k, _):
                o = at(k // 2, k % 2, oc)
                self.copy(o, 3, core).wait_recv()
                return 0

            lax.fori_loop(0, n // 2, arrive, 0)

        def drain(self):
            def sent(k, _):
                o = at(k, y, c)

                @pl.when(jnp.logical_and(has_up, k <= z))
                def _():
                    self.copy(o, 0, up).wait_send()

                @pl.when(jnp.logical_and(has_down, k >= z))
                def _():
                    self.copy(o, 1, down).wait_send()

                self.copy(o, 2, side).wait_send()
                self.copy(o, 3, core).wait_send()
                self.copy(at(k, oy, c), 3, core).wait_send()
                return 0

            lax.fori_loop(0, H, sent, 0)

    items = Gather(gi, ib, agi_s, agi_r)
    users = Gather(gu, ub, agu_s, agu_r)
    items.first()
    for load in loads:
        load.start()

    zero = jnp.zeros((K, T), BF16)
    for b in range(ub):
        x = uf_ref[pl.ds(b * T, T), :]
        t = jnp.transpose(x)
        utf[pl.ds(b * K, K), :] = t
        t = t.astype(BF16)
        gu[me * ub + b] = t
        uto[b] = t
        unat[b] = x.astype(BF16)
    gi[n * ib] = zero
    scaled[ub] = zero
    items.step(1)
    users.first()
    lent = jnp.transpose(len_ref[0].astype(F32))
    for g in range(R // GROUP):
        lens[g] = lent[:, g * GROUP:(g + 1) * GROUP]
    run[0] = jnp.zeros((K, T), F32)
    uacc[...] = jnp.zeros(uacc.shape, F32)
    pacc[...] = jnp.zeros(pacc.shape, F32)
    for t in range(2, H):
        items.step(t)
    items.finish()
    for load in loads[:parts]:
        load.wait()

    columns = lax.broadcasted_iota(jnp.int32, (T, T), 1).astype(F32)
    every = (R // GROUP) // H

    def rate(g, _):
        @pl.when(jnp.logical_and(g % every == 0, g // every + 1 < H))
        def _():
            users.step(g // every + 1)

        cut = lens[g]
        errs = []
        picks = []
        for j in range(GROUP):
            r = g * GROUP + j
            u = ruser[0, r]
            i = ritem[0, r]
            pred = jnp.dot(unat[u], gi[i], preferred_element_type=F32)
            e = jnp.where(columns < cut[:, j:j + 1], pred - rat[r].astype(F32), 0.0).astype(BF16)
            errs.append(e)
            picks.append(jnp.concatenate(
                [gi[jnp.where(u == b, i, n * ib)] for b in range(ub)], axis=0))
            term = jnp.dot(uto[u], e, preferred_element_type=F32)
            run[r + 1] = term + run[links[r]]
        uacc[...] += lax.dot_general(
            jnp.concatenate(picks, axis=1), jnp.concatenate(errs, axis=1), NT,
            preferred_element_type=F32)
        return 0

    lax.fori_loop(0, R // GROUP, rate, 0)

    class Reduce:
        def __init__(self, buf, width, rc, ry, ru, rd, own, cs, cr, ys, yr, zs, zr):
            self.buf, self.width, self.own = buf, width, own
            self.rc, self.ry, self.ru, self.rd = rc, ry, ru, rd
            self.cs, self.cr, self.ys, self.yr, self.zs, self.zr = cs, cr, ys, yr, zs, zr

        def cross(self, zz, yy):
            k = zz * 2 + yy
            return remote(self.buf.at[at(zz, yy, oc)], self.rc.at[k], self.cs.at[k], self.cr.at[k], core)

        def aside(self, zz):
            return remote(self.buf.at[at(zz, oy, c)], self.ry.at[zz], self.ys.at[zz], self.yr.at[zz], side)

        def climb(self, zz):
            return remote(self.buf.at[at(zz, y, c)], self.ru.at[zz], self.zs.at[zz], self.zr.at[0, zz], up)

        def sink(self, zz):
            return remote(self.buf.at[at(zz, y, c)], self.rd.at[zz], self.zs.at[zz], self.zr.at[1, zz], down)

        def turn(self, zz):
            self.cross(zz, oy).wait_recv()
            d = at(zz, oy, c)
            self.buf[d] = (self.buf[d].astype(F32) + self.rc[zz * 2 + oy].astype(F32)).astype(BF16)
            self.aside(zz).start()

        def line(self, zz):
            d = at(zz, y, c)
            self.cross(zz, y).wait_recv()
            self.aside(zz).wait_recv()
            self.own[...] = (self.buf[d].astype(F32) + self.rc[zz * 2 + y].astype(F32)
                             + self.ry[zz].astype(F32))

            @pl.when(jnp.logical_and(z <= zz, has_down))
            def _():
                self.climb(zz).wait_recv()
                self.own[...] += self.ru[zz].astype(F32)

            @pl.when(jnp.logical_and(z >= zz, has_up))
            def _():
                self.sink(zz).wait_recv()
                self.own[...] += self.rd[zz].astype(F32)

            @pl.when(z != zz)
            def _():
                self.buf[d] = self.own[...].astype(BF16)

            @pl.when(z < zz)
            def _():
                self.climb(zz).start()

            @pl.when(z > zz)
            def _():
                self.sink(zz).start()

            @pl.when(z == zz)
            def _():
                self.buf_own[...] = self.own[...]

        def drain(self):
            def sent(k, _):
                self.cross(k, 0).wait_send()
                self.cross(k, 1).wait_send()
                self.aside(k).wait_send()

                @pl.when(z < k)
                def _():
                    self.climb(k).wait_send()

                @pl.when(z > k)
                def _():
                    self.sink(k).wait_send()

                return 0

            lax.fori_loop(0, H, sent, 0)

    item_sum = Reduce(ci, ib, ric, riy, riu, rid, own_i.at[0], ici_s, ici_r, iy_s, iy_r, iz_s, iz_r)
    item_sum.buf_own = own_i.at[1]
    user_sum = Reduce(cu, ub, ruc, ruy, ruu, rud, own_u.at[0], uci_s, uci_r, uy_s, uy_r, uz_s, uz_r)
    user_sum.buf_own = own_u.at[1]

    def order(k):
        odd = k % 2
        return (1 - odd) * (H - 1 - k // 2) + odd * (k // 2)

    def fill(d):
        for b in range(ib):
            ci[d, pl.ds(b * K, K), :] = run[links[R + d * ib + b]].astype(BF16)

    def fill_other(k, _):
        for yy in (oy, y):
            fill(at(order(k), yy, oc))
            item_sum.cross(order(k), yy).start()
        return 0

    def fill_mine(k, _):
        for yy in (oy, y):
            fill(at(order(k), yy, c))
        return 0

    lax.fori_loop(0, H, fill_other, 0)
    lax.fori_loop(0, H, fill_mine, 0)
    users.finish()
    gu[n * ub] = zero
    for load in loads[parts:]:
        load.wait()

    row = lax.broadcasted_iota(jnp.int32, (16, T), 0)

    def pull(p, _):
        @pl.when(jnp.logical_and(p >= n - H, p < n))
        def _():
            item_sum.turn(order(p - (n - H)))

        lhs = []
        rhs = []
        for k in range(cap):
            s = tsrc[0, p, k]
            t = p * ub + tdst[0, p, k]
            ones = jnp.where(row == s, 1.0, 0.0).astype(BF16)
            lhs.append(jnp.concatenate(
                [gu[jnp.where(s == b, t, n * ub)] for b in range(ub)] + [ones], axis=0))
            rhs.append(w[p * cap + k])
        pacc[...] += lax.dot_general(
            jnp.concatenate(lhs, axis=1), jnp.concatenate(rhs, axis=1), NT,
            preferred_element_type=F32)
        return 0

    lax.fori_loop(0, n, pull, 0)
    for b in range(ub):
        den = 1.0 + pacc[ub * K + b:ub * K + b + 1, :]
        rows = pl.ds(b * K, K)
        err = utf[rows, :] - pacc[rows, :] / den
        pe[rows, :] = err
        scaled[b] = (err / den).astype(BF16)

    def give(p):
        lhs = []
        for k in range(cap):
            s = tsrc[0, p, k]
            t = tdst[0, p, k]
            lhs.append(jnp.concatenate(
                [scaled[jnp.where(t == b, s, ub)] for b in range(ub)], axis=0))
        tiles = w[pl.ds(p * cap, cap)].reshape(cap * T, T)
        cu[p] = jnp.dot(jnp.concatenate(lhs, axis=1), tiles, preferred_element_type=F32).astype(BF16)

    def give_other(k, _):
        zz = order(k % H)
        yy = (k // H) * y + (1 - k // H) * oy
        give(at(zz, yy, oc))
        user_sum.cross(zz, yy).start()
        return 0

    def give_side(k, _):
        zz = order(k)
        give(at(zz, oy, c))
        user_sum.turn(zz)
        return 0

    def give_mine(k, _):
        give(at(order(k), y, c))
        item_sum.line(order(k))
        return 0

    def user_line(k, _):
        user_sum.line(order(k))
        return 0

    lax.fori_loop(0, 2 * H, give_other, 0)
    lax.fori_loop(0, H, give_side, 0)
    lax.fori_loop(0, H, give_mine, 0)
    for b in range(ib):
        rows = pl.ds(b * K, K)
        ig_ref[pl.ds(b * T, T), :] = jnp.transpose(own_i[1, rows, :] + reg_coef * itf[rows, :])
    lax.fori_loop(0, H, user_line, 0)
    for b in range(ub):
        rows = pl.ds(b * K, K)
        total = (uacc[rows, :] + social_coef * (pe[rows, :] - own_u[1, rows, :])
                 + reg_coef * utf[rows, :])
        ug_ref[pl.ds(b * T, T), :] = jnp.transpose(total)
    items.drain()
    users.drain()
    item_sum.drain()
    user_sum.drain()


def body(n, user_factors, item_factors, ratings, rating_len, rating_user, rating_item,
         trust_src, trust_dst, trust_weight):
    T = ratings.shape[-1]
    K = user_factors.shape[1]
    ub = user_factors.shape[0] // T
    ib = item_factors.shape[0] // T
    R = ratings.shape[1]
    cap = trust_src.shape[2]
    H = n // 4
    tile_items = rating_item[0]
    ids = jnp.concatenate([tile_items, jnp.arange(n * ib, dtype=jnp.int32)])
    limit = jnp.minimum(jnp.arange(R + n * ib, dtype=jnp.int32), R)
    at = jnp.arange(R, dtype=jnp.int32)
    links = jnp.max(jnp.where((ids[:, None] == tile_items[None, :]) & (at[None, :] < limit[:, None]),
                              at[None, :] + 1, 0), axis=1)
    weights = trust_weight.reshape(n * cap, T, T)
    vmem = pl.BlockSpec(memory_space=pltpu.VMEM)
    smem = pl.BlockSpec(memory_space=pltpu.SMEM)
    hbm = pl.BlockSpec(memory_space=pl.ANY)
    dma = pltpu.SemaphoreType.DMA
    scratch = [
        pltpu.VMEM((R, T, T), BF16),
        pltpu.VMEM((n * cap, T, T), BF16),
        pltpu.VMEM((n * ib + 1, K, T), BF16),
        pltpu.VMEM((n * ub + 1, K, T), BF16),
        pltpu.VMEM((ub, T, K), BF16),
        pltpu.VMEM((ub * K, T), F32),
        pltpu.VMEM((ib * K, T), F32),
        pltpu.VMEM((ub, K, T), BF16),
        pltpu.VMEM((R // GROUP, T, GROUP), F32),
        pltpu.VMEM((R + 1, K, T), F32),
        pltpu.VMEM((ub * K, T), F32),
        pltpu.VMEM((ub * K + 16, T), F32),
        pltpu.VMEM((ub * K, T), F32),
        pltpu.VMEM((ub + 1, K, T), BF16),
    ]
    for width in (ib, ub):
        scratch += [pltpu.VMEM((count, width * K, T), BF16) for count in (n, n // 2, H, H, H)]
    scratch += [pltpu.VMEM((2, width * K, T), F32) for width in (ib, ub)]
    scratch += [dma((8,)), dma((4, n)), dma((n,)), dma((4, n)), dma((n,))]
    for _ in range(2):
        scratch += [dma((n // 2,)), dma((n // 2,)), dma((H,)), dma((H,)), dma((H,)), dma((2, H))]
    return pl.pallas_call(
        functools.partial(kernel, n),
        out_shape=(jax.ShapeDtypeStruct(user_factors.shape, F32),
                   jax.ShapeDtypeStruct(item_factors.shape, F32)),
        in_specs=[vmem, vmem, hbm, vmem, smem, smem, smem, smem, hbm, smem],
        out_specs=(vmem, vmem),
        scratch_shapes=scratch,
        compiler_params=pltpu.CompilerParams(
            collective_id=0, has_side_effects=True, vmem_limit_bytes=56 * 1024 * 1024),
    )(user_factors, item_factors, ratings, rating_len, rating_user, rating_item,
      trust_src, trust_dst, weights, links)


def solution(mesh):
    row = P(("parts", "user"))
    return jax.shard_map(
        functools.partial(body, mesh.shape["user"]), mesh=mesh,
        in_specs=(row,) * 9, out_specs=(row, row), check_vma=False)
```

time: 176 us -> 128 us (0.73)
  the two profiles are of different devices: /device:TPU:0 before, /device:TPU:8 now
where the time goes in v1:
time: 128 us; the launch traced here: 127 us
  Pallas kernels  115 us (90%)
  local copies, waits for them, and re-layouts  10 us (8%)
  other arithmetic  2.01 us (2%)
    pallas_call x1, Pallas kernels, body(): pl.pallas_call(functools.partial(kernel, n), out_shape=(jax.ShapeDtypeStr...  115 us
    unnamed x4, local copies, waits for them, and re-layouts  6.39 us
    pallas_call x2, local copies, waits for them, and re-layouts, body(): pl.pallas_call(functools.partial(kernel, n), out_shape=(jax.ShapeDtypeStr...  3.65 us

profile of v1, /device:TPU:8, one launch (start us, length us, event | category | flops | bytes accessed | tf_op | source)
XLA Modules:
  0.0 127.5 jit_solution(314436945990646069)
XLA Ops:
  0.6 0.7 pad_add_fusion
  1.4 1.3 %select_reduce_fusion.links = s32[96]{0:T(128)} fusion(s32[64]{0:T(128)S(1)} %iota_add_fusion, s32[96]{0:T(128)S(1)} %get-tuple-element.7, s32[96]{0:T(128)S(1)} %get-tuple-element.6, s32[64]{0:T(128)} %bitcast.4), kind=kLoop, calls=%fused_computation | loop fusion | flops 30624 | bytes 1664 | tf_op jit(solution)/shard_map/reduce_max | solution.py:439
  2.7 1.4 %copy.19.tsrc = s32[1,16,3]{2,1,0:T(8,128)} copy(s32[1,16,3]{1,0,2:T(1,128)} %param.15) | data formatting | bytes 384 | tf_op args[6]
  4.0 1.4 %copy.20.tdst = s32[1,16,3]{2,1,0:T(8,128)} copy(s32[1,16,3]{1,0,2:T(1,128)} %param.16) | data formatting | bytes 384 | tf_op args[7]
  5.4 1.7 %copy.18.if_ref = f32[512,64]{1,0:T(8,128)} copy(f32[512,64]{0,1:T(8,128)} %param.10) | data formatting | bytes 262144 | tf_op args[1]
  7.1 1.9 %copy.17.uf_ref = f32[1024,64]{1,0:T(8,128)} copy(f32[1024,64]{0,1:T(8,128)} %param.9) | data formatting | bytes 524288 | tf_op args[0]
  9.0 114.8 %shard_map.104 = (f32[1024,64]{1,0:T(8,128)}, f32[512,64]{1,0:T(8,128)}) custom-call(f32[1024,64]{1,0:T(8,128)} %copy.17.uf_ref, f32[512,64]{1,0:T(8,128)} %copy.18.if_ref, bf16[1,64,256,256]{3,2,1,0:T(8,128)(2,1)} %rat_hbm.1, s32[1,64,256]{2,1,0:T(8,128)} %len_ref.1, s32[1,64]{1,0:T(1,128)} %ruser.1, s32[1,64]{1,0:T(1,128)} %ritem.1, ...), custom_call_target="tpu_custom_call" | custom-call | tf_op jit(solution)/shard_map/pallas_call | solution.py:468
  123.8 1.9 %copy.21 = f32[1024,64]{0,1:T(8,128)} copy(f32[1024,64]{1,0:T(8,128)} %get-tuple-element.4) | data formatting | bytes 524288 | tf_op jit(solution)/shard_map/pallas_call | solution.py:468
  125.8 1.7 %copy.22 = f32[512,64]{0,1:T(8,128)} copy(f32[512,64]{1,0:T(8,128)} %get-tuple-element.5) | data formatting | bytes 262144 | tf_op jit(solution)/shard_map/pallas_call | solution.py:468
  (2 shorter events, 0.0 us)

commit v2 on v1

--- a/solution.py
+++ b/solution.py
@@ -31,10 +31,9 @@
     c = me % 2
     oc = 1 - c
     oy = 1 - y
-    T = uf_ref.shape[0] // unat.shape[0]
-    K = uf_ref.shape[1]
+    K, T = uto.shape[1:]
     ub = unat.shape[0]
-    ib = if_ref.shape[0] // T
+    ib = if_ref.shape[1] // T
     R = rat.shape[0]
     cap = w.shape[0] // n
 
@@ -65,7 +64,7 @@
         loads.append(pltpu.make_async_copy(w_hbm.at[wide], w.at[wide], load_sem.at[parts + q]))
 
     for b in range(ib):
-        t = jnp.transpose(if_ref[pl.ds(b * T, T), :])
+        t = if_ref[:, pl.ds(b * T, T)]
         itf[pl.ds(b * K, K), :] = t
         gi[me * ib + b] = t.astype(BF16)
 
@@ -185,13 +184,12 @@
 
     zero = jnp.zeros((K, T), BF16)
     for b in range(ub):
-        x = uf_ref[pl.ds(b * T, T), :]
-        t = jnp.transpose(x)
+        t = uf_ref[:, pl.ds(b * T, T)]
+        unat[b] = jnp.transpose(t).astype(BF16)
         utf[pl.ds(b * K, K), :] = t
         t = t.astype(BF16)
         gu[me * ub + b] = t
         uto[b] = t
-        unat[b] = x.astype(BF16)
     gi[n * ib] = zero
     scaled[ub] = zero
     items.step(1)
@@ -318,9 +316,15 @@
     user_sum = Reduce(cu, ub, ruc, ruy, ruu, rud, own_u.at[0], uci_s, uci_r, uy_s, uy_r, uz_s, uz_r)
     user_sum.buf_own = own_u.at[1]
 
+    low = (2 * z < H).astype(jnp.int32)
+
     def order(k):
-        odd = k % 2
-        return (1 - odd) * (H - 1 - k // 2) + odd * (k // 2)
+        last = (k == H - 1).astype(jnp.int32)
+        near = (k < H - 1 - z).astype(jnp.int32)
+        far = (k < z).astype(jnp.int32)
+        rising = near * (H - 1 - k) + (1 - near) * (k - (H - 1 - z))
+        falling = far * k + (1 - far) * (H - 1 - (k - z))
+        return last * z + (1 - last) * (low * rising + (1 - low) * falling)
 
     def fill(d):
         for b in range(ib):
@@ -354,8 +358,8 @@
         lhs = []
         rhs = []
         for k in range(cap):
-            s = tsrc[0, p, k]
-            t = p * ub + tdst[0, p, k]
+            s = tsrc[k, 0, p]
+            t = p * ub + tdst[k, 0, p]
             ones = jnp.where(row == s, 1.0, 0.0).astype(BF16)
             lhs.append(jnp.concatenate(
                 [gu[jnp.where(s == b, t, n * ub)] for b in range(ub)] + [ones], axis=0))
@@ -376,8 +380,8 @@
     def give(p):
         lhs = []
         for k in range(cap):
-            s = tsrc[0, p, k]
-            t = tdst[0, p, k]
+            s = tsrc[k, 0, p]
+            t = tdst[k, 0, p]
             lhs.append(jnp.concatenate(
                 [scaled[jnp.where(t == b, s, ub)] for b in range(ub)], axis=0))
         tiles = w[pl.ds(p * cap, cap)].reshape(cap * T, T)
@@ -410,13 +414,13 @@
     lax.fori_loop(0, H, give_mine, 0)
     for b in range(ib):
         rows = pl.ds(b * K, K)
-        ig_ref[pl.ds(b * T, T), :] = jnp.transpose(own_i[1, rows, :] + reg_coef * itf[rows, :])
+        ig_ref[:, pl.ds(b * T, T)] = own_i[1, rows, :] + reg_coef * itf[rows, :]
     lax.fori_loop(0, H, user_line, 0)
     for b in range(ub):
         rows = pl.ds(b * K, K)
         total = (uacc[rows, :] + social_coef * (pe[rows, :] - own_u[1, rows, :])
                  + reg_coef * utf[rows, :])
-        ug_ref[pl.ds(b * T, T), :] = jnp.transpose(total)
+        ug_ref[:, pl.ds(b * T, T)] = total
     items.drain()
     users.drain()
     item_sum.drain()
@@ -465,17 +469,18 @@
     scratch += [dma((8,)), dma((4, n)), dma((n,)), dma((4, n)), dma((n,))]
     for _ in range(2):
         scratch += [dma((n // 2,)), dma((n // 2,)), dma((H,)), dma((H,)), dma((H,)), dma((2, H))]
-    return pl.pallas_call(
+    user_grad, item_grad = pl.pallas_call(
         functools.partial(kernel, n),
-        out_shape=(jax.ShapeDtypeStruct(user_factors.shape, F32),
-                   jax.ShapeDtypeStruct(item_factors.shape, F32)),
+        out_shape=(jax.ShapeDtypeStruct((K, ub * T), F32),
+                   jax.ShapeDtypeStruct((K, ib * T), F32)),
         in_specs=[vmem, vmem, hbm, vmem, smem, smem, smem, smem, hbm, smem],
         out_specs=(vmem, vmem),
         scratch_shapes=scratch,
         compiler_params=pltpu.CompilerParams(
             collective_id=0, has_side_effects=True, vmem_limit_bytes=56 * 1024 * 1024),
-    )(user_factors, item_factors, ratings, rating_len, rating_user, rating_item,
-      trust_src, trust_dst, weights, links)
+    )(user_factors.T, item_factors.T, ratings, rating_len, rating_user, rating_item,
+      trust_src.transpose(2, 0, 1), trust_dst.transpose(2, 0, 1), weights, links)
+    return user_grad.T, item_grad.T
 
 
 def solution(mesh):

time: 128 us -> 82 us (0.64)
  the two profiles are of different devices: /device:TPU:8 before, /device:TPU:0 now
where the time goes in v2:
time: 82 us; the launch traced here: 81.8 us
  Pallas kernels  75.9 us (93%)
  local copies, waits for them, and re-layouts  3.24 us (4%)
  other arithmetic  2 us (2%)
    pallas_call x1, Pallas kernels, body(): pl.pallas_call(functools.partial(kernel, n), out_shape=(jax.ShapeDtypeStr...  75.9 us
    unnamed x2, local copies, waits for them, and re-layouts  3.24 us

profile of v2, /device:TPU:0, one launch (start us, length us, event | category | flops | bytes accessed | tf_op | source)
XLA Modules:
  0.0 81.8 jit_solution(9071868029381732563)
XLA Ops:
  0.6 0.7 pad_add_fusion
  1.4 1.3 %select_reduce_fusion.links = s32[96]{0:T(128)} fusion(s32[64]{0:T(128)S(1)} %iota_add_fusion, s32[96]{0:T(128)S(1)} %get-tuple-element.7, s32[96]{0:T(128)S(1)} %get-tuple-element.6, s32[64]{0:T(128)} %bitcast.14), kind=kLoop, calls=%fused_computation | loop fusion | flops 30624 | bytes 1664 | tf_op jit(solution)/shard_map/reduce_max | solution.py:443
  2.6 75.9 %shard_map.104 = (f32[64,1024]{1,0:T(8,128)}, f32[64,512]{1,0:T(8,128)}) custom-call(f32[64,1024]{1,0:T(8,128)} %bitcast.9, f32[64,512]{1,0:T(8,128)} %bitcast.11, bf16[1,64,256,256]{3,2,1,0:T(8,128)(2,1)} %rat_hbm.1, s32[1,64,256]{2,1,0:T(8,128)} %len_ref.1, s32[1,64]{1,0:T(1,128)} %ruser.1, s32[1,64]{1,0:T(1,128)} %ritem.1, s32[3,1,16]{2,1,0:T(1,128)} %bitcast.15, ...), custom_call_target="tpu_custom_call" | custom-call | tf_op jit(solution)/shard_map/pallas_call | solution.py:472
  78.5 1.7 %copy.13 = f32[1024,64]{0,1:T(8,128)} copy(f32[1024,64]{0,1:T(8,128)} %bitcast.10) | data formatting | bytes 524288
  80.2 1.6 %copy.14 = f32[512,64]{0,1:T(8,128)} copy(f32[512,64]{0,1:T(8,128)} %bitcast.12) | data formatting | bytes 262144
  (2 shorter events, 0.0 us)

commit v3 on v2

--- a/solution.py
+++ b/solution.py
@@ -18,7 +18,7 @@
 def kernel(
     n, uf_ref, if_ref, rat_hbm, len_ref, ruser, ritem, tsrc, tdst, w_hbm, links,
     ug_ref, ig_ref,
-    rat, w, gi, gu, unat, utf, itf, uto, lens, run, uacc, pacc, pe, scaled,
+    rat, w, gi, gu, unat, utf, itf, uto, lens, run, uacc, pacc, pe, scaled, held,
     ci, ric, riy, riu, rid, cu, ruc, ruy, ruu, rud, own_i, own_u,
     load_sem, agi_s, agi_r, agu_s, agu_r,
     ici_s, ici_r, iy_s, iy_r, iz_s, iz_r,
@@ -209,31 +209,52 @@
     columns = lax.broadcasted_iota(jnp.int32, (T, T), 1).astype(F32)
     every = (R // GROUP) // H
 
-    def rate(g, _):
-        @pl.when(jnp.logical_and(g % every == 0, g // every + 1 < H))
-        def _():
-            users.step(g // every + 1)
-
+    def predict(g):
         cut = lens[g]
         errs = []
+        for j in range(GROUP):
+            r = g * GROUP + j
+            pred = jnp.dot(unat[ruser[0, r]], gi[ritem[0, r]], preferred_element_type=F32)
+            errs.append(jnp.where(
+                columns < cut[:, j:j + 1], pred - rat[r].astype(F32), 0.0).astype(BF16))
+        return errs
+
+    def spread(g, errs):
         picks = []
+        terms = []
         for j in range(GROUP):
             r = g * GROUP + j
             u = ruser[0, r]
             i = ritem[0, r]
-            pred = jnp.dot(unat[u], gi[i], preferred_element_type=F32)
-            e = jnp.where(columns < cut[:, j:j + 1], pred - rat[r].astype(F32), 0.0).astype(BF16)
-            errs.append(e)
             picks.append(jnp.concatenate(
                 [gi[jnp.where(u == b, i, n * ib)] for b in range(ub)], axis=0))
-            term = jnp.dot(uto[u], e, preferred_element_type=F32)
-            run[r + 1] = term + run[links[r]]
+            terms.append(jnp.dot(uto[u], errs[j], preferred_element_type=F32))
         uacc[...] += lax.dot_general(
             jnp.concatenate(picks, axis=1), jnp.concatenate(errs, axis=1), NT,
             preferred_element_type=F32)
-        return 0
-
-    lax.fori_loop(0, R // GROUP, rate, 0)
+        for j in range(GROUP):
+            r = g * GROUP + j
+            run[r + 1] = terms[j] + run[links[r]]
+
+    def travel(g):
+        @pl.when(jnp.logical_and(g % every == 0, g // every + 1 < H))
+        def _():
+            users.step(g // every + 1)
+
+    def keep(g):
+        for j, e in enumerate(predict(g)):
+            held[j] = e
+
+    def rate(g, _):
+        travel(g)
+        spread(g - 1, [held[j] for j in range(GROUP)])
+        keep(g)
+        return 0
+
+    travel(0)
+    keep(0)
+    lax.fori_loop(1, R // GROUP, rate, 0)
+    spread(R // GROUP - 1, [held[j] for j in range(GROUP)])
 
     class Reduce:
         def __init__(self, buf, width, rc, ry, ru, rd, own, cs, cr, ys, yr, zs, zr):
@@ -337,8 +358,9 @@
         return 0
 
     def fill_mine(k, _):
-        for yy in (oy, y):
-            fill(at(order(k), yy, c))
+        fill(at(order(k), oy, c))
+        item_sum.turn(order(k))
+        fill(at(order(k), y, c))
         return 0
 
     lax.fori_loop(0, H, fill_other, 0)
@@ -351,9 +373,9 @@
     row = lax.broadcasted_iota(jnp.int32, (16, T), 0)
 
     def pull(p, _):
-        @pl.when(jnp.logical_and(p >= n - H, p < n))
+        @pl.when(p > n - H)
         def _():
-            item_sum.turn(order(p - (n - H)))
+            item_sum.line(order(p - (n - H) - 1))
 
         lhs = []
         rhs = []
@@ -387,12 +409,11 @@
         tiles = w[pl.ds(p * cap, cap)].reshape(cap * T, T)
         cu[p] = jnp.dot(jnp.concatenate(lhs, axis=1), tiles, preferred_element_type=F32).astype(BF16)
 
-    def give_other(k, _):
-        zz = order(k % H)
-        yy = (k // H) * y + (1 - k // H) * oy
+    def give_across(k, yy):
+        zz = order(k)
         give(at(zz, yy, oc))
         user_sum.cross(zz, yy).start()
-        return 0
+        return yy
 
     def give_side(k, _):
         zz = order(k)
@@ -402,16 +423,17 @@
 
     def give_mine(k, _):
         give(at(order(k), y, c))
-        item_sum.line(order(k))
         return 0
 
     def user_line(k, _):
         user_sum.line(order(k))
         return 0
 
-    lax.fori_loop(0, 2 * H, give_other, 0)
+    lax.fori_loop(0, H, give_across, oy)
     lax.fori_loop(0, H, give_side, 0)
+    lax.fori_loop(0, H, give_across, y)
     lax.fori_loop(0, H, give_mine, 0)
+    item_sum.line(z)
     for b in range(ib):
         rows = pl.ds(b * K, K)
         ig_ref[:, pl.ds(b * T, T)] = own_i[1, rows, :] + reg_coef * itf[rows, :]
@@ -462,6 +484,7 @@
         pltpu.VMEM((ub * K + 16, T), F32),
         pltpu.VMEM((ub * K, T), F32),
         pltpu.VMEM((ub + 1, K, T), BF16),
+        pltpu.VMEM((GROUP, T, T), BF16),
     ]
     for width in (ib, ub):
         scratch += [pltpu.VMEM((count, width * K, T), BF16) for count in (n, n // 2, H, H, H)]

time: 82 us -> 72.8 us (0.89)
  Pallas kernels: 75.9 us -> 66.7 us
    pallas_call x1, Pallas kernels: 75.9 us -> 66.7 us  [body(): pl.pallas_call(functools.partial(kernel, n), out_shape=(jax.ShapeDtypeStr...]
where the time goes in v3:
time: 72.8 us; the launch traced here: 72.6 us
  Pallas kernels  66.7 us (92%)
  local copies, waits for them, and re-layouts  3.24 us (4%)
  other arithmetic  2 us (3%)
    pallas_call x1, Pallas kernels, body(): pl.pallas_call(functools.partial(kernel, n), out_shape=(jax.ShapeDtypeStr...  66.7 us
    unnamed x2, local copies, waits for them, and re-layouts  3.24 us

profile of v3, /device:TPU:0, one launch (start us, length us, event | category | flops | bytes accessed | tf_op | source)
XLA Modules:
  0.0 72.6 jit_solution(1938327916017967425)
XLA Ops:
  0.6 0.7 %pad_add_fusion = (s32[96]{0:T(128)S(1)}, s32[96]{0:T(128)S(1)}) fusion(s32[32]{0:T(128)S(1)} %iota.15, s32[64]{0:T(128)} %bitcast.13), kind=kLoop, calls=%fused_computation.3 | loop fusion | flops 192 | bytes 1152 | tf_op jit(solution)/shard_map/concatenate | solution.py:462
  1.4 1.3 %select_reduce_fusion.links = s32[96]{0:T(128)} fusion(s32[64]{0:T(128)S(1)} %iota_add_fusion, s32[96]{0:T(128)S(1)} %get-tuple-element.7, s32[96]{0:T(128)S(1)} %get-tuple-element.6, s32[64]{0:T(128)} %bitcast.14), kind=kLoop, calls=%fused_computation | loop fusion | flops 30624 | bytes 1664 | tf_op jit(solution)/shard_map/reduce_max | solution.py:465
  2.6 66.7 %shard_map.104 = (f32[64,1024]{1,0:T(8,128)}, f32[64,512]{1,0:T(8,128)}) custom-call(f32[64,1024]{1,0:T(8,128)} %bitcast.9, f32[64,512]{1,0:T(8,128)} %bitcast.11, bf16[1,64,256,256]{3,2,1,0:T(8,128)(2,1)} %rat_hbm.1, s32[1,64,256]{2,1,0:T(8,128)} %len_ref.1, s32[1,64]{1,0:T(1,128)} %ruser.1, s32[1,64]{1,0:T(1,128)} %ritem.1, s32[3,1,16]{2,1,0:T(1,128)} %bitcast.15, ...), custom_call_target="tpu_custom_call" | custom-call | tf_op jit(solution)/shard_map/pallas_call | solution.py:495
  69.4 1.7 %copy.13 = f32[1024,64]{0,1:T(8,128)} copy(f32[1024,64]{0,1:T(8,128)} %bitcast.10) | data formatting | bytes 524288
  71.0 1.6 %copy.14 = f32[512,64]{0,1:T(8,128)} copy(f32[512,64]{0,1:T(8,128)} %bitcast.12) | data formatting | bytes 262144
  (2 shorter events, 0.0 us)
